TPU v7x, 512 devices: a whole 4x8x8 slice. The times are simulated.
512 devices in a mesh: dp: 64 (over z_lo, y, x), emb: 8 (over z_hi, core).
Axes of the slice: x: 4, y: 8, z: 8 (z_hi: 4, z_lo: 2; z = z_hi * 2 + z_lo), core: 2. Of those that a mesh axis runs over, the one named last changes fastest.
Arguments:
- image_emb: bfloat16 [1152, 16384], P('emb', 'dp'), may hold values from -6 to 6
- text_feat: bfloat16 [1152, 16384], P(None, 'dp'), may hold values from -6 to 6
- head_weight: bfloat16 [1152, 1152], P('emb'), may hold values from -0.1875 to 0.1875
- logit_scale: float32 [1], replicated, may hold values from 4 to 16
- logit_bias: float32 [1], replicated, may hold values from -3 to -1
Outputs:
- image_grad: bfloat16 [1152, 16384], P('emb', 'dp')
- head_grad: float32 [1152, 1152], P('emb')
All inputs are finite; a program needn't handle non-finite values.
Results may differ from a plain program's by a relative error of at most 0.022.
Values may be sent and summed in bfloat16 or wider, within the bound.
A program may use at most 64 MiB of HBM per device.

v0:
```python
import jax
import jax.numpy as jnp
from jax import lax
from jax.sharding import PartitionSpec as P

REACH = 6


EPSILON = 1e-06


def shifted(block, axis, distance):
    devices = range(lax.axis_size(axis))
    route = [((i - distance) % len(devices), i) for i in devices]
    return lax.ppermute(block, axis, route)


def on_device(image_emb, text_feat, head_weight, logit_scale, logit_bias):
    local = image_emb.astype(jnp.float32)
    text_raw = jnp.dot(head_weight, text_feat, preferred_element_type=jnp.float32)
    lengths = lax.psum((jnp.sum(local * local, 0), jnp.sum(text_raw * text_raw, 0)), "emb")
    image_len = jnp.sqrt(lengths[0] + EPSILON)
    text_len = jnp.sqrt(lengths[1] + EPSILON)
    image_unit = (local / image_len).astype(jnp.bfloat16)
    text_unit = (text_raw / text_len).astype(jnp.bfloat16)
    scale = logit_scale[0]
    offset = logit_bias[0]
    count = image_emb.shape[1]

    def cosines(blocks):
        partial_value = lax.dot_general(
            image_unit, blocks, (((0,), (0,)), ((), ())), preferred_element_type=jnp.float32
        )
        return lax.psum(partial_value.astype(jnp.bfloat16), "emb").astype(jnp.float32)

    def tile_grads(blocks, diagonal):
        cosine = cosines(blocks)
        logits = scale * cosine + offset
        row_ids = jnp.arange(count, dtype=jnp.int32)
        col_ids = jnp.arange(blocks.shape[1], dtype=jnp.int32) % count
        same = (row_ids[:, None] == col_ids[None, :]) & diagonal
        sign = jnp.where(same, jnp.float32(1.0), jnp.float32(-1.0))
        weights = (-scale * sign * jax.nn.sigmoid(-sign * logits)).astype(jnp.bfloat16)
        image_part = lax.dot_general(
            blocks, weights, (((1,), (1,)), ((), ())), preferred_element_type=jnp.float32
        )
        text_part = jnp.dot(image_unit, weights, preferred_element_type=jnp.float32)
        return (image_part, text_part)

    first = shifted(text_unit, "dp", REACH)
    first_image, first_text = tile_grads(first, jnp.bool_(REACH == 0))

    def turn(index, carry):
        block, total, image_dir = carry
        block = shifted(block, "dp", -1)
        total = shifted(total.astype(jnp.bfloat16), "dp", -1).astype(total.dtype)
        image_part, text_part = tile_grads(block, index == REACH - 1)
        return (block, total + text_part, image_dir + image_part)

    block, total, image_dir = lax.fori_loop(0, 2 * REACH, turn, (first, first_text, first_image))
    text_dir = shifted(total.astype(jnp.bfloat16), "dp", REACH).astype(total.dtype)
    image_f = image_unit.astype(jnp.float32)
    text_f = text_unit.astype(jnp.float32)
    inner = lax.psum((jnp.sum(image_f * image_dir, 0), jnp.sum(text_f * text_dir, 0)), "emb")
    image_grad = ((image_dir - image_f * inner[0]) / image_len).astype(jnp.bfloat16)
    text_grad = ((text_dir - text_f * inner[1]) / text_len).astype(jnp.bfloat16)
    head_part = lax.dot_general(
        text_grad, text_feat, (((1,), (1,)), ((), ())), preferred_element_type=jnp.float32
    )
    head_grad = lax.psum(head_part, "dp")
    return (image_grad, head_grad)


def solution(mesh):
    placed = (P("emb", "dp"), P(None, "dp"), P("emb", None), P(), P())
    return jax.shard_map(
        on_device,
        mesh=mesh,
        in_specs=placed,
        out_specs=(P("emb", "dp"), P("emb", None)),
        check_vma=False,
    )
```

profile of v0, /device:TPU:1, one launch (start us, length us, event | category | flops | bytes accessed | tf_op | source)
XLA Modules:
  0.0 1762.9 jit_solution(11269300175493926406)
XLA Ops:
  9.5 20.5 %all-reduce.1 = (f32[256]{0:T(256)S(1)}, f32[256]{0:T(256)S(1)}) all-reduce(f32[256]{0:T(256)S(1)} %get-tuple-element.208, f32[256]{0:T(256)S(1)} %fusion.13), channel_id=1, replica_groups=mesh['dp'=64,'emb'=8] {'emb'}, use_global_device_ids=true, to_apply=%region_1.0 | all-reduce | flops 512 | bytes 4096 | tf_op jit(solution)/shard_map/psum | solution.py:21
  30.0 5.6 collective-permute-start.2
  35.7 5.4 collective-permute-done.2
  43.3 75.0 %all-reduce.6.cloned.1.call-done = bf16[256,256]{1,0:T(8,128)(2,1)} async-done(((bf16[256,256]{1,0:T(8,128)(2,1)}), bf16[256,256]{1,0:T(8,128)(2,1)}) %all-reduce.6.cloned.1.call-update) | async-done | bytes 131088 | tf_op jit(solution)/shard_map/psum | solution.py:34
  119.6 1070.2 %while.19 = (s32[]{:T(128)}, bf16[144,256]{1,0:T(8,128)(2,1)S(1)}, bf16[144,256]{1,0:T(8,128)(2,1)S(1)}, f32[144,256]{1,0:T(8,128)S(1)}, f32[]{:T(128)}, /*index...) while((s32[]{:T(128)}, bf16[144,256]{1,0:T(8,128)(2,1)S(1)}, ...), condition=%wide.region_7.8_spmd, body=%wide.region_5.7_spmd.sunk | while | flops 58738176 | bytes 3181852 | solution.py:60
  119.7 6.8 collective-permute-start
  128.8 7.9 collective-permute-start.1
  138.1 66.6 %all-reduce.10.cloned.1.call-done = bf16[256,256]{1,0:T(8,128)(2,1)} async-done(((bf16[256,256]{1,0:T(8,128)(2,1)}), bf16[256,256]{1,0:T(8,128)(2,1)}) %all-reduce.10.cloned.1.call-update) | async-done | bytes 131088 | tf_op jit(solution)/shard_map/while/body/eval_jaxpr/psum | solution.py:34
  204.7 2.5 convert_add_fusion.2
  208.9 6.8 collective-permute-start
  218.0 7.9 collective-permute-start.1
  227.3 66.6 %all-reduce.10.cloned.1.call-done = bf16[256,256]{1,0:T(8,128)(2,1)} async-done(((bf16[256,256]{1,0:T(8,128)(2,1)}), bf16[256,256]{1,0:T(8,128)(2,1)}) %all-reduce.10.cloned.1.call-update) | async-done | bytes 131088 | tf_op jit(solution)/shard_map/while/body/eval_jaxpr/psum | solution.py:34
  293.9 2.5 convert_add_fusion.2
  296.5 1.6 fusion.54
  298.2 6.8 collective-permute-start
  307.2 7.9 collective-permute-start.1
  316.6 66.5 %all-reduce.10.cloned.1.call-done = bf16[256,256]{1,0:T(8,128)(2,1)} async-done(((bf16[256,256]{1,0:T(8,128)(2,1)}), bf16[256,256]{1,0:T(8,128)(2,1)}) %all-reduce.10.cloned.1.call-update) | async-done | bytes 131088 | tf_op jit(solution)/shard_map/while/body/eval_jaxpr/psum | solution.py:34
  383.1 2.5 convert_add_fusion.2
  387.3 6.8 collective-permute-start
  396.4 7.9 collective-permute-start.1
  405.7 66.6 %all-reduce.10.cloned.1.call-done = bf16[256,256]{1,0:T(8,128)(2,1)} async-done(((bf16[256,256]{1,0:T(8,128)(2,1)}), bf16[256,256]{1,0:T(8,128)(2,1)}) %all-reduce.10.cloned.1.call-update) | async-done | bytes 131088 | tf_op jit(solution)/shard_map/while/body/eval_jaxpr/psum | solution.py:34
  472.3 2.5 convert_add_fusion.2
  474.8 1.6 fusion.54
  476.5 6.8 collective-permute-start
  485.6 7.9 collective-permute-start.1
  494.9 66.6 %all-reduce.10.cloned.1.call-done = bf16[256,256]{1,0:T(8,128)(2,1)} async-done(((bf16[256,256]{1,0:T(8,128)(2,1)}), bf16[256,256]{1,0:T(8,128)(2,1)}) %all-reduce.10.cloned.1.call-update) | async-done | bytes 131088 | tf_op jit(solution)/shard_map/while/body/eval_jaxpr/psum | solution.py:34
  561.5 2.5 convert_add_fusion.2
  565.7 6.8 collective-permute-start
  574.8 7.9 collective-permute-start.1
  584.1 66.6 %all-reduce.10.cloned.1.call-done = bf16[256,256]{1,0:T(8,128)(2,1)} async-done(((bf16[256,256]{1,0:T(8,128)(2,1)}), bf16[256,256]{1,0:T(8,128)(2,1)}) %all-reduce.10.cloned.1.call-update) | async-done | bytes 131088 | tf_op jit(solution)/shard_map/while/body/eval_jaxpr/psum | solution.py:34
  650.7 2.5 convert_add_fusion.2
  654.9 6.8 collective-permute-start
  664.0 7.9 collective-permute-start.1
  673.3 66.5 %all-reduce.10.cloned.1.call-done = bf16[256,256]{1,0:T(8,128)(2,1)} async-done(((bf16[256,256]{1,0:T(8,128)(2,1)}), bf16[256,256]{1,0:T(8,128)(2,1)}) %all-reduce.10.cloned.1.call-update) | async-done | bytes 131088 | tf_op jit(solution)/shard_map/while/body/eval_jaxpr/psum | solution.py:34
  739.8 2.5 convert_add_fusion.2
  742.4 1.6 fusion.54
  744.0 6.8 collective-permute-start
  753.1 7.9 collective-permute-start.1
  762.4 66.6 %all-reduce.10.cloned.1.call-done = bf16[256,256]{1,0:T(8,128)(2,1)} async-done(((bf16[256,256]{1,0:T(8,128)(2,1)}), bf16[256,256]{1,0:T(8,128)(2,1)}) %all-reduce.10.cloned.1.call-update) | async-done | bytes 131088 | tf_op jit(solution)/shard_map/while/body/eval_jaxpr/psum | solution.py:34
  829.0 2.5 convert_add_fusion.2
  831.5 1.6 fusion.54
  833.2 6.8 collective-permute-start
  842.3 7.9 collective-permute-start.1
  851.6 66.6 %all-reduce.10.cloned.1.call-done = bf16[256,256]{1,0:T(8,128)(2,1)} async-done(((bf16[256,256]{1,0:T(8,128)(2,1)}), bf16[256,256]{1,0:T(8,128)(2,1)}) %all-reduce.10.cloned.1.call-update) | async-done | bytes 131088 | tf_op jit(solution)/shard_map/while/body/eval_jaxpr/psum | solution.py:34
  918.2 2.5 convert_add_fusion.2
  920.7 1.6 fusion.54
  922.4 6.8 collective-permute-start
  931.5 7.9 collective-permute-start.1
  940.8 66.6 %all-reduce.10.cloned.1.call-done = bf16[256,256]{1,0:T(8,128)(2,1)} async-done(((bf16[256,256]{1,0:T(8,128)(2,1)}), bf16[256,256]{1,0:T(8,128)(2,1)}) %all-reduce.10.cloned.1.call-update) | async-done | bytes 131088 | tf_op jit(solution)/shard_map/while/body/eval_jaxpr/psum | solution.py:34
  1007.4 2.5 convert_add_fusion.2
  1011.6 6.8 collective-permute-start
  1020.7 7.9 collective-permute-start.1
  1030.0 66.6 %all-reduce.10.cloned.1.call-done = bf16[256,256]{1,0:T(8,128)(2,1)} async-done(((bf16[256,256]{1,0:T(8,128)(2,1)}), bf16[256,256]{1,0:T(8,128)(2,1)}) %all-reduce.10.cloned.1.call-update) | async-done | bytes 131088 | tf_op jit(solution)/shard_map/while/body/eval_jaxpr/psum | solution.py:34
  1096.5 2.5 convert_add_fusion.2
  1099.1 1.6 fusion.54
  1100.8 6.8 collective-permute-start
  1109.8 7.9 collective-permute-start.1
  1119.2 66.6 %all-reduce.10.cloned.1.call-done = bf16[256,256]{1,0:T(8,128)(2,1)} async-done(((bf16[256,256]{1,0:T(8,128)(2,1)}), bf16[256,256]{1,0:T(8,128)(2,1)}) %all-reduce.10.cloned.1.call-update) | async-done | bytes 131088 | tf_op jit(solution)/shard_map/while/body/eval_jaxpr/psum | solution.py:34
  1185.7 2.5 convert_add_fusion.2
  1189.9 5.5 collective-permute-start.3
  1195.5 5.7 collective-permute-done.3
  1201.3 16.6 all-reduce
  1219.8 534.6 %all-reduce.8.cloned.1.call-done = f32[144,1152]{1,0:T(8,128)} async-done(((f32[144,1152]{1,0:T(8,128)}), f32[144,1152]{1,0:T(8,128)}) %all-reduce.8.cloned.1.call-update) | async-done | bytes 663568 | tf_op jit(solution)/shard_map/psum | solution.py:70
  1754.4 2.0 copy.26
  (136 shorter events, 60.7 us)
Async XLA Ops:
  7.2 1.1 copy-start
  7.2 111.1 %all-reduce.6.cloned.1.call-start = ((), (), s32[]{:S(2)}) async-start(), calls=%async_computation | async-start | bytes 262144 | tf_op jit(solution)/shard_map/psum | solution.py:34
  30.0 5.6 copy-start.1
  30.0 11.0 collective-permute-start.2
  119.6 85.1 %all-reduce.10.cloned.1.call-start = ((), (), s32[]{:S(2)}) async-start(), calls=%async_computation.2 | async-start | bytes 262144 | tf_op jit(solution)/shard_map/while/body/eval_jaxpr/psum | solution.py:34
  119.7 8.2 collective-permute-start
  128.8 9.3 collective-permute-start.1
  204.7 2.5 copy-start.2
  208.9 85.1 %all-reduce.10.cloned.1.call-start = ((), (), s32[]{:S(2)}) async-start(), calls=%async_computation.2 | async-start | bytes 262144 | tf_op jit(solution)/shard_map/while/body/eval_jaxpr/psum | solution.py:34
  208.9 8.2 collective-permute-start
  218.0 9.3 collective-permute-start.1
  293.9 2.5 copy-start.2
  298.1 85.0 %all-reduce.10.cloned.1.call-start = ((), (), s32[]{:S(2)}) async-start(), calls=%async_computation.2 | async-start | bytes 262144 | tf_op jit(solution)/shard_map/while/body/eval_jaxpr/psum | solution.py:34
  298.2 8.2 collective-permute-start
  307.2 9.3 collective-permute-start.1
  383.1 2.5 copy-start.2
  387.3 85.0 %all-reduce.10.cloned.1.call-start = ((), (), s32[]{:S(2)}) async-start(), calls=%async_computation.2 | async-start | bytes 262144 | tf_op jit(solution)/shard_map/while/body/eval_jaxpr/psum | solution.py:34
  387.3 8.2 collective-permute-start
  396.4 9.3 collective-permute-start.1
  472.3 2.5 copy-start.2
  476.5 85.0 %all-reduce.10.cloned.1.call-start = ((), (), s32[]{:S(2)}) async-start(), calls=%async_computation.2 | async-start | bytes 262144 | tf_op jit(solution)/shard_map/while/body/eval_jaxpr/psum | solution.py:34
  476.5 8.2 collective-permute-start
  485.6 9.3 collective-permute-start.1
  561.5 2.5 copy-start.2
  565.7 85.0 %all-reduce.10.cloned.1.call-start = ((), (), s32[]{:S(2)}) async-start(), calls=%async_computation.2 | async-start | bytes 262144 | tf_op jit(solution)/shard_map/while/body/eval_jaxpr/psum | solution.py:34
  565.7 8.2 collective-permute-start
  574.8 9.3 collective-permute-start.1
  650.7 2.5 copy-start.2
  654.8 85.0 %all-reduce.10.cloned.1.call-start = ((), (), s32[]{:S(2)}) async-start(), calls=%async_computation.2 | async-start | bytes 262144 | tf_op jit(solution)/shard_map/while/body/eval_jaxpr/psum | solution.py:34
  654.9 8.2 collective-permute-start
  664.0 9.3 collective-permute-start.1
  739.8 2.5 copy-start.2
  744.0 85.0 %all-reduce.10.cloned.1.call-start = ((), (), s32[]{:S(2)}) async-start(), calls=%async_computation.2 | async-start | bytes 262144 | tf_op jit(solution)/shard_map/while/body/eval_jaxpr/psum | solution.py:34
  744.0 8.2 collective-permute-start
  753.1 9.3 collective-permute-start.1
  829.0 2.5 copy-start.2
  833.2 85.0 %all-reduce.10.cloned.1.call-start = ((), (), s32[]{:S(2)}) async-start(), calls=%async_computation.2 | async-start | bytes 262144 | tf_op jit(solution)/shard_map/while/body/eval_jaxpr/psum | solution.py:34
  833.2 8.2 collective-permute-start
  842.3 9.3 collective-permute-start.1
  918.2 2.5 copy-start.2
  922.4 85.0 %all-reduce.10.cloned.1.call-start = ((), (), s32[]{:S(2)}) async-start(), calls=%async_computation.2 | async-start | bytes 262144 | tf_op jit(solution)/shard_map/while/body/eval_jaxpr/psum | solution.py:34
  922.4 8.2 collective-permute-start
  931.5 9.3 collective-permute-start.1
  1007.4 2.5 copy-start.2
  1011.5 85.0 %all-reduce.10.cloned.1.call-start = ((), (), s32[]{:S(2)}) async-start(), calls=%async_computation.2 | async-start | bytes 262144 | tf_op jit(solution)/shard_map/while/body/eval_jaxpr/psum | solution.py:34
  1011.6 8.2 collective-permute-start
  1020.7 9.3 collective-permute-start.1
  1096.5 2.5 copy-start.2
  1100.7 85.0 %all-reduce.10.cloned.1.call-start = ((), (), s32[]{:S(2)}) async-start(), calls=%async_computation.2 | async-start | bytes 262144 | tf_op jit(solution)/shard_map/while/body/eval_jaxpr/psum | solution.py:34
  1100.8 8.2 collective-permute-start
  1109.8 9.3 collective-permute-start.1
  1185.7 2.5 copy-start.2
  1189.9 564.5 %all-reduce.8.cloned.1.call-start = ((), (), s32[]{:S(2)}) async-start(), calls=%async_computation.1 | async-start | bytes 1327104 | tf_op jit(solution)/shard_map/psum | solution.py:70
  1189.9 11.3 collective-permute-start.3
Sparse Core Ops, SparseCore 0:
  42.1 76.1 all-reduce.5
  128.9 75.7 all-reduce.9
  218.1 75.7 all-reduce.9
  307.4 75.6 all-reduce.9
  396.5 75.7 all-reduce.9
  485.7 75.7 all-reduce.9
  574.9 75.7 all-reduce.9
  664.1 75.6 all-reduce.9
  753.3 75.7 all-reduce.9
  842.4 75.7 all-reduce.9
  931.6 75.7 all-reduce.9
  1020.8 75.7 all-reduce.9
  1110.0 75.7 all-reduce.9
  1219.2 535.1 all-reduce.7
where the time goes:
time: 1800 us; the launch traced here: 1760 us
  waiting for transfers between devices  1450 us (81%)
  starting transfers between devices  188 us (10%)
  matrix products  63.9 us (4%)
  blocking collectives  37.1 us (2%)
    psum x13, waiting for transfers between devices, cosines(): lax.psum(partial_value.astype(jnp.bfloat16), 'emb').astype(jnp.float32)  874 us
    psum x1, waiting for transfers between devices, on_device(): head_grad = lax.psum(head_part, 'dp')  535 us
    ppermute x26, starting transfers between devices, shifted(): return lax.ppermute(block, axis, route)  188 us
    ppermute x26, waiting for transfers between devices, shifted(): return lax.ppermute(block, axis, route)  44 us
  transfers between devices with their start and end apart: 40, of which 40 were waited for; matrix products, arithmetic and copies ran while one was open for 0% of the time, Pallas kernels for 0%

commit v1 on v0

v1 whole, which is shorter than its diff:
```python
import functools

import jax
import jax.numpy as jnp
from jax import lax
from jax.experimental import pallas as pl
from jax.experimental.pallas import tpu as pltpu
from jax.sharding import PartitionSpec as P

REACH = 6
EPSILON = 1e-06
N_ZLO, N_Y, N_X = 2, 8, 4
LANES = 128
ORDER = (0, 1, -1, 4, -4, 3, -3, 2, -2, 5, -5, 6, -6)
SLOT = {o: i for i, o in enumerate(ORDER)}
NEAR, MIDDLE = 7, 11
MESH = pl.DeviceIdType.MESH
BF16, F32 = jnp.bfloat16, jnp.float32


def up(value, step):
    return -(-value // step) * step


def kernel(
    sizes,
    image_hbm,
    feat_hbm,
    weight_hbm,
    scale_ref,
    bias_ref,
    image_out,
    head_out,
    image_ref,
    feat_ref,
    weight_ref,
    turn_f,
    swap_src,
    swap_dst,
    images,
    text_nat,
    text,
    weights,
    grad,
    text_part,
    pair_dst,
    line_src,
    line_dst,
    mid_dst,
    dirs,
    dirs_back,
    back_src,
    back_dst,
    head_src,
    head_dst,
    col_src,
    col_dst,
    col_sum,
    head_sum,
    load,
    swap_s,
    swap_r,
    win_s,
    win_r,
    gat_s,
    gat_r,
    fwd_s,
    fwd_r,
    pair_s,
    pair_r,
    line_s,
    line_r,
    mid_s,
    mid_r,
    ret_s,
    ret_r,
    back_s,
    back_r,
    head_s,
    head_r,
    col_s,
    col_r,
    cga_s,
    cga_r,
    hga_s,
    hga_r,
):
    n_dp, n_emb, depth, pairs, width, chunk, piece = sizes
    tail = depth - LANES
    rows = pairs // n_emb
    n_hi = n_emb // 2
    n_group, n_col = N_ZLO * N_X, N_Y
    wide = LANES * n_emb + LANES
    slots = 2 * REACH + 1
    me = lax.axis_index("dp")
    k = lax.axis_index("emb")
    hi, core = k // 2, k % 2
    x_at, y_at, z_at = me % N_X, (me // N_X) % N_Y, me // (N_X * N_Y)
    first_group = (z_at * N_X + x_at) * (1 - core) + y_at * core
    second_group = y_at * (1 - core) + (z_at * N_X + x_at) * core

    def emb_peer(m):
        return (me, (k + m) % n_emb)

    def dp_peer(offset):
        return ((me + offset + n_dp) % n_dp, k)

    partner = (me, k + 1 - 2 * core)

    def hi_of(m):
        return (hi + m) % n_hi

    def line_peer(m):
        return (me, 2 * hi_of(m) + core)

    def chip_at(plane, line):
        return (plane // N_X) * (N_X * N_Y) + line * N_X + plane % N_X

    def group_of(m):
        return (first_group + m) % n_group

    def group_peer(m):
        to = group_of(m)
        here, there = chip_at(to, y_at), chip_at(z_at * N_X + x_at, to)
        return (here * (1 - core) + there * core, k)

    def col_of(m):
        return (second_group + m) % n_col

    def col_peer(m):
        to = col_of(m)
        here, there = chip_at(z_at * N_X + x_at, to), chip_at(to, y_at)
        return (here * (1 - core) + there * core, k)

    def at16(start, size):
        return pl.ds(pl.multiple_of(start, 16), size)

    def push(src, dst, send, recv, peer):
        copy = pltpu.make_async_remote_copy(
            src_ref=src,
            dst_ref=dst,
            send_sem=send,
            recv_sem=recv,
            device_id=peer,
            device_id_type=MESH,
        )
        copy.start()
        return copy

    def slot(o):
        return pl.ds(rows * SLOT[o], rows)

    def loaded(i, src, dst):
        copy = pltpu.make_async_copy(src, dst, load.at[i])
        copy.start()
        return copy

    loads = [
        loaded(0, image_hbm, image_ref),
        loaded(1, weight_hbm, weight_ref),
        loaded(2, feat_hbm, feat_ref),
    ]

    greeted = (
        [emb_peer(m) for m in (4, 3, 5, 2, 6, 1, 7)]
        + [dp_peer(o) for o in (1, -1, N_X, -N_X, N_X - 1, 1 - N_X, N_X + 1, -N_X - 1)]
        + [group_peer(m) for m in range(1, n_group)]
        + [col_peer(m) for m in range(1, n_col)]
    )
    barrier = pltpu.get_barrier_semaphore()
    for peer in greeted:
        pl.semaphore_signal(barrier, inc=1, device_id=peer, device_id_type=MESH)

    turn_f[LANES:, :] = jnp.zeros((LANES, pairs), F32)
    loads[0].wait()
    turn_f[:LANES, :] = image_ref[:LANES, :].astype(F32)
    turn_f[pl.ds(pl.multiple_of(LANES + tail * k, 16), tail), :] = image_ref[LANES:, :].astype(F32)
    swap_src[...] = jnp.transpose(turn_f[...]).astype(BF16)
    swap_dst[pl.ds(k, 1)] = swap_src[at16(rows * k, rows), :][None]
    pl.semaphore_wait(barrier, len(greeted))

    swaps = [
        push(
            swap_src.at[at16(rows * ((k + m) % n_emb), rows), :],
            swap_dst.at[k],
            swap_s.at[m],
            swap_r.at[m],
            emb_peer(m),
        )
        for m in range(1, n_emb)
    ]
    own_text = at16(depth * k, depth)
    loads[1].wait()
    loads[2].wait()
    text_nat[own_text, :] = jnp.dot(
        weight_ref[...], feat_ref[...], preferred_element_type=F32
    ).astype(BF16)

    upper, lower = line_peer(1), line_peer(n_hi - 1)
    cut = up(depth // 2, 16)
    gathers = [
        push(text_nat.at[own_text, :], text_nat.at[own_text, :], gat_s.at[0], gat_r.at[0], upper),
        push(text_nat.at[own_text, :], text_nat.at[own_text, :], gat_s.at[1], gat_r.at[1], lower),
    ]
    forwards = [
        push(text_nat.at[own_text, :], text_nat.at[own_text, :], fwd_s.at[0], fwd_r.at[0], partner)
    ]

    for copy in swaps:
        copy.wait_recv()
    raw = [swap_dst[j, :, :LANES].astype(F32) for j in range(n_emb)]
    raw.append(sum(swap_dst[j, :, LANES:].astype(F32) for j in range(n_emb)))
    square = sum(jnp.sum(r * r, axis=1, keepdims=True) for r in raw)
    image_inv = 1.0 / jnp.sqrt(square + EPSILON)
    home = slot(0)
    for j, r in enumerate(raw):
        images[home, LANES * j : LANES * (j + 1)] = (r * image_inv).astype(BF16)
    window = {}

    def pass_on(have, o):
        window[o] = push(
            images.at[slot(have), :],
            images.at[slot(o), :],
            win_s.at[SLOT[o]],
            win_r.at[SLOT[o]],
            dp_peer(have - o),
        )

    for o in (1, -1, N_X, -N_X, N_X - 1, 1 - N_X):
        pass_on(0, o)

    below = at16(depth * (2 * ((hi + n_hi - 1) % n_hi) + core), depth)
    above = at16(depth * (2 * ((hi + 1) % n_hi) + core), depth)
    across = depth * (2 * ((hi + 2) % n_hi) + core)
    below_cut = at16(depth * (2 * ((hi + n_hi - 1) % n_hi) + core), cut)
    above_cut = at16(depth * (2 * ((hi + 1) % n_hi) + core) + cut, depth - cut)
    gathers[0].wait_recv()
    gathers.append(
        push(text_nat.at[below_cut, :], text_nat.at[below_cut, :], gat_s.at[2], gat_r.at[2], upper)
    )
    gathers[1].wait_recv()
    gathers.append(
        push(text_nat.at[above_cut, :], text_nat.at[above_cut, :], gat_s.at[3], gat_r.at[3], lower)
    )
    for i, come in ((1, below), (2, above)):
        forwards.append(
            push(text_nat.at[come, :], text_nat.at[come, :], fwd_s.at[i], fwd_r.at[i], partner)
        )

    for near in (1, -1):
        window[near].wait_recv()
        for o in (N_X + 2, N_X + 1, 2):
            pass_on(near, near * o)

    gathers[2].wait_recv()
    gathers[3].wait_recv()
    come = at16(across, depth)
    forwards.append(
        push(text_nat.at[come, :], text_nat.at[come, :], fwd_s.at[3], fwd_r.at[3], partner)
    )

    for copy in forwards:
        copy.wait_recv()
    if LANES > tail * n_emb:
        text[LANES * n_emb + tail * n_emb :, :] = jnp.zeros((LANES - tail * n_emb, pairs), BF16)
    square = jnp.zeros((1, pairs), F32)
    for j in range(n_emb):
        part = text_nat[depth * j : depth * (j + 1), :]
        text[LANES * j : LANES * (j + 1), :] = part[:LANES]
        text[LANES * n_emb + tail * j : LANES * n_emb + tail * (j + 1), :] = part[LANES:]
        wide_part = part.astype(F32)
        square = square + jnp.sum(wide_part * wide_part, axis=0, keepdims=True)
    text_inv = 1.0 / jnp.sqrt(square + EPSILON)

    scale, bias = scale_ref[0], bias_ref[0]

    def meet(first, last):
        at = pl.ds(rows * first, rows * (last - first))
        cosine = jnp.dot(images[at, :], text[...], preferred_element_type=F32) * text_inv
        logits = scale * cosine + bias
        if first == 0:
            row_ids = lax.broadcasted_iota(jnp.int32, logits.shape, 0)
            col_ids = lax.broadcasted_iota(jnp.int32, logits.shape, 1)
            same = (row_ids < rows) & (col_ids - rows * k == row_ids)
            sign = jnp.where(same, jnp.float32(1.0), jnp.float32(-1.0))
        else:
            sign = jnp.float32(-1.0)
        sig = 1.0 / (1.0 + jnp.exp(sign * logits))
        value = (-scale * sign * sig * text_inv).astype(BF16)
        weights[at, :] = value
        return jnp.sum(value.astype(F32) * cosine, axis=0, keepdims=True)

    def turn_back(first, last):
        at = pl.ds(rows * first, rows * (last - first))
        dirs[at, :] = lax.dot_general(
            weights[at, :], text[...], (((1,), (1,)), ((), ())), preferred_element_type=F32
        ).astype(BF16)

    def text_side(first, last):
        at = pl.ds(rows * first, rows * (last - first))
        return lax.dot_general(
            images[at, :], weights[at, :], (((0,), (0,)), ((), ())), preferred_element_type=F32
        )

    for o in ORDER[3:NEAR]:
        window[o].wait_recv()
    inner = meet(0, NEAR)
    for o in ORDER[NEAR:MIDDLE]:
        window[o].wait_recv()
    inner = inner + meet(NEAR, MIDDLE)
    grad[...] = text_side(0, MIDDLE)
    for o in ORDER[MIDDLE:]:
        window[o].wait_recv()
    inner = (inner + meet(MIDDLE, len(ORDER))) * text_inv

    late = text_side(MIDDLE, len(ORDER))
    for j in range(n_emb):
        for at, size, to in ((LANES * j, LANES, 0), (LANES * n_emb + tail * j, tail, LANES)):
            part = grad[at : at + size, :] + late[at : at + size]
            part = part - text[at : at + size, :].astype(F32) * inner
            text_part[depth * j + to : depth * j + to + size, :] = part.astype(BF16)
    paired = {}
    for m in (2, 1, 3, 0):
        theirs = at16(depth * (2 * hi_of(m) + 1 - core), depth)
        paired[m] = push(text_part.at[theirs, :], pair_dst.at[m], pair_s.at[m], pair_r.at[m], partner)

    turn_back(0, len(ORDER))
    returns = {}

    def give_back(o, step):
        returns[o] = push(
            dirs.at[slot(o), :],
            dirs_back.at[slot(o), :],
            ret_s.at[SLOT[o]],
            ret_r.at[SLOT[o]],
            dp_peer(step),
        )

    def collect(o, sources):
        value = dirs[slot(o), :].astype(F32)
        for source in sources:
            returns[source].wait_recv()
            value = value + dirs_back[slot(source), :].astype(F32)
        return value

    def summed(m):
        paired[m].wait_recv()
        mine = at16(depth * (2 * hi_of(m) + core), depth)
        return text_part[mine, :].astype(F32) + pair_dst[m].astype(F32)

    first, second = pl.ds(0, cut), pl.ds(cut, depth - cut)
    line_src[0] = summed(2).astype(BF16)
    lines = [
        push(line_src.at[0, first, :], mid_dst.at[first, :], mid_s.at[0], mid_r.at[0], upper),
        push(line_src.at[0, second, :], mid_dst.at[second, :], mid_s.at[1], mid_r.at[1], lower),
    ]
    rising, falling = summed(1), summed(3)
    line_src[1, cut:, :] = rising[cut:].astype(BF16)
    line_src[2, :cut, :] = falling[:cut].astype(BF16)

    def line(i, j, part, peer):
        return push(line_src.at[i, part, :], line_dst.at[i, part, :], line_s.at[j], line_r.at[j], peer)

    lines.append(line(1, 0, second, upper))
    lines.append(line(2, 1, first, lower))
    lines[0].wait_recv()
    line_src[1, :cut, :] = (rising[:cut] + mid_dst[:cut, :].astype(F32)).astype(BF16)
    lines.append(line(1, 2, first, upper))
    lines[1].wait_recv()
    line_src[2, cut:, :] = (falling[cut:] + mid_dst[cut:, :].astype(F32)).astype(BF16)
    lines.append(line(2, 3, second, lower))
    for way in (1, -1):
        give_back(5 * way, N_X * way)
        give_back(3 * way, (N_X - 1) * way)
        give_back(6 * way, (N_X + 1) * way)
        give_back(2 * way, way)
        give_back(4 * way, N_X * way)
    for copy in swaps + gathers + forwards + list(window.values()):
        copy.wait_send()
    total = summed(0)
    for copy in lines[2:]:
        copy.wait_recv()
    total = total + line_dst[1].astype(F32) + line_dst[2].astype(F32)

    share = lax.dot_general(
        total.astype(BF16), feat_ref[...], (((1,), (1,)), ((), ())), preferred_element_type=F32
    )
    tiles = width // LANES
    for c in range(tiles):
        head_src[depth * c : depth * (c + 1), :] = share[:, LANES * c : LANES * (c + 1)].astype(BF16)
    if chunk * n_group > depth * tiles:
        head_src[depth * tiles :, :] = jnp.zeros((chunk * n_group - depth * tiles, LANES), BF16)
    heads = [
        push(
            head_src.at[at16(chunk * group_of(m), chunk), :],
            head_dst.at[m],
            head_s.at[m],
            head_r.at[m],
            group_peer(m),
        )
        for m in range(1, n_group)
    ]

    for way in (1, -1):
        dirs[slot(way), :] = collect(way, (2 * way, 5 * way, 6 * way)).astype(BF16)
        give_back(way, way)

    total = head_src[at16(chunk * first_group, chunk), :].astype(F32)
    for m in range(1, n_group):
        heads[m - 1].wait_recv()
        total = total + head_dst[m].astype(F32)
    col_src[:chunk, :] = total.astype(BF16)
    if piece * n_col > chunk:
        col_src[chunk:, :] = jnp.zeros((piece * n_col - chunk, LANES), BF16)
    cols = [
        push(col_src.at[at16(piece * col_of(m), piece), :], col_dst.at[m], col_s.at[m], col_r.at[m], col_peer(m))
        for m in range(1, n_col)
    ]

    for copy in lines + list(paired.values()) + heads:
        copy.wait_send()
    way = collect(0, (1, -1, 3, -3, 4, -4))
    unit = images[home, :].astype(F32)
    along = jnp.sum(unit * way, axis=1, keepdims=True)
    image_grad = ((way - unit * along) * image_inv).astype(BF16)
    for j in range(n_emb):
        back_src[j, :, :LANES] = image_grad[:, LANES * j : LANES * (j + 1)]
        back_src[j, :, LANES:] = image_grad[:, LANES * n_emb :]
    own_rows = at16(rows * k, rows)
    backs = [
        push(back_src.at[(k + m) % n_emb], back_dst.at[own_rows, :], back_s.at[m], back_r.at[m], emb_peer(m))
        for m in range(1, n_emb)
    ]
    back_dst[own_rows, :] = back_src[pl.ds(k, 1)][0]

    own_piece = at16(piece * second_group, piece)
    total = col_src[own_piece, :].astype(F32)
    for m in range(1, n_col):
        cols[m - 1].wait_recv()
        total = total + col_dst[m].astype(F32)
    col_sum[own_piece, :] = total.astype(BF16)
    col_gathers = [
        push(col_sum.at[own_piece, :], col_sum.at[own_piece, :], cga_s.at[m], cga_r.at[m], col_peer(m))
        for m in range(1, n_col)
    ]
    for copy in col_gathers:
        copy.wait_recv()
    own_chunk = at16(chunk * first_group, chunk)
    head_sum[own_chunk, :] = col_sum[:chunk, :]
    head_gathers = [
        push(col_sum.at[pl.ds(0, chunk), :], head_sum.at[own_chunk, :], hga_s.at[m], hga_r.at[m], group_peer(m))
        for m in range(1, n_group)
    ]

    for copy in backs:
        copy.wait_recv()
    turn_f[...] = jnp.transpose(back_dst[...].astype(F32))
    image_out[:LANES, :] = turn_f[:LANES, :].astype(BF16)
    image_out[LANES:, :] = turn_f[pl.ds(pl.multiple_of(LANES + tail * k, 16), tail), :].astype(BF16)

    for copy in list(returns.values()) + backs + cols + col_gathers:
        copy.wait_send()
    for copy in head_gathers:
        copy.wait_recv()
    for c in range(tiles):
        head_out[:, LANES * c : LANES * (c + 1)] = head_sum[depth * c : depth * (c + 1), :]

    for copy in head_gathers:
        copy.wait_send()


def on_device(image_emb, text_feat, head_weight, logit_scale, logit_bias):
    n_dp, n_emb = lax.axis_size("dp"), lax.axis_size("emb")
    depth, pairs = image_emb.shape
    width = text_feat.shape[0]
    rows = pairs // n_emb
    n_hi = n_emb // 2
    n_group, n_col = N_ZLO * N_X, N_Y
    slots = 2 * REACH + 1
    wide = LANES * n_emb + LANES
    chunk = up(depth * (width // LANES), 16 * n_group) // n_group
    piece = up(chunk, 16 * n_col) // n_col
    sizes = (n_dp, n_emb, depth, pairs, width, chunk, piece)
    scratch = [
        pltpu.VMEM((depth, pairs), BF16),
        pltpu.VMEM((width, pairs), BF16),
        pltpu.VMEM((depth, width), BF16),
        pltpu.VMEM((2 * LANES, pairs), F32),
        pltpu.VMEM((pairs, 2 * LANES), BF16),
        pltpu.VMEM((n_emb, rows, 2 * LANES), BF16),
        pltpu.VMEM((rows * slots, wide), BF16),
        pltpu.VMEM((depth * n_emb, pairs), BF16),
        pltpu.VMEM((wide, pairs), BF16),
        pltpu.VMEM((rows * slots, pairs), BF16),
        pltpu.VMEM((wide, pairs), F32),
        pltpu.VMEM((depth * n_emb, pairs), BF16),
        pltpu.VMEM((n_hi, depth, pairs), BF16),
        pltpu.VMEM((3, depth, pairs), BF16),
        pltpu.VMEM((3, depth, pairs), BF16),
        pltpu.VMEM((depth, pairs), BF16),
        pltpu.VMEM((rows * slots, wide), BF16),
        pltpu.VMEM((rows * slots, wide), BF16),
        pltpu.VMEM((n_emb, rows, 2 * LANES), BF16),
        pltpu.VMEM((pairs, 2 * LANES), BF16),
        pltpu.VMEM((chunk * n_group, LANES), BF16),
        pltpu.VMEM((n_group, chunk, LANES), BF16),
        pltpu.VMEM((piece * n_col, LANES), BF16),
        pltpu.VMEM((n_col, piece, LANES), BF16),
        pltpu.VMEM((piece * n_col, LANES), BF16),
        pltpu.VMEM((chunk * n_group, LANES), BF16),
    ]
    scratch.append(pltpu.SemaphoreType.DMA((3,)))
    for count in (n_emb, slots, 4, 4, n_hi, 4, 2, slots, n_emb, n_group, n_col, n_col, n_group):
        scratch += [pltpu.SemaphoreType.DMA((count,))] * 2
    hbm = pl.BlockSpec(memory_space=pltpu.HBM)
    smem = pl.BlockSpec(memory_space=pltpu.SMEM)
    vmem = pl.BlockSpec(memory_space=pltpu.VMEM)
    inputs = [
        pltpu.with_memory_space_constraint(x, pltpu.HBM)
        for x in (image_emb, text_feat, head_weight)
    ]
    image_grad, head_grad = pl.pallas_call(
        functools.partial(kernel, sizes),
        out_shape=(
            jax.ShapeDtypeStruct((depth, pairs), BF16),
            jax.ShapeDtypeStruct((depth, width), BF16),
        ),
        in_specs=[hbm, hbm, hbm, smem, smem],
        out_specs=(vmem, vmem),
        scratch_shapes=scratch,
        compiler_params=pltpu.CompilerParams(
            collective_id=0, has_side_effects=True, vmem_limit_bytes=40 * 1024 * 1024
        ),
    )(*inputs, logit_scale, logit_bias)
    return image_grad, head_grad.astype(F32)


def solution(mesh):
    placed = (P("emb", "dp"), P(None, "dp"), P("emb", None), P(), P())
    return jax.shard_map(
        on_device,
        mesh=mesh,
        in_specs=placed,
        out_specs=(P("emb", "dp"), P("emb", None)),
        check_vma=False,
    )
```

time: 1800 us -> 80.2 us (0.04); the launches traced: 1760 us -> 80 us
  waiting for transfers between devices: 1450 us -> 0 us
  starting transfers between devices: 188 us -> 0 us
  Pallas kernels: 0 us -> 76.6 us
  matrix products: 63.9 us -> 0 us
  blocking collectives: 37.1 us -> 0 us
    psum x14 -> x0, waiting for transfers between devices: 1410 us -> none  [the longest x13 874 us: cosines(): lax.psum(partial_value.astype(jnp.bfloat16), 'emb').astype(jnp.float32)]
    ppermute x26 -> x0, starting transfers between devices: 188 us -> none  [shifted(): return lax.ppermute(block, axis, route)]
    pallas_call x0 -> x1, Pallas kernels: none -> 76.6 us  [on_device(): pl.pallas_call(functools.partial(kernel, sizes), out_shape=(jax.ShapeDtyp...]
    dot_general x41 -> x0, matrix products: 63.9 us -> none  [the longest x13 30.5 us: tile_grads(): text_part = jnp.dot(image_unit, weights, preferred_element_type=jnp.float32)]
    ppermute x26 -> x0, waiting for transfers between devices: 44 us -> none  [shifted(): return lax.ppermute(block, axis, route)]
    psum x2 -> x0, blocking collectives: 37.1 us -> none  [the longest x1 20.5 us: on_device(): lax.psum((jnp.sum(local * local, 0), jnp.sum(text_raw * text_raw, 0)), 'e...]
  transfers between devices with their start and end apart: 40 -> 0, of which waited for: 40 -> 0; matrix products, arithmetic and copies ran while one was open for 0% -> 0% of each run, Pallas kernels for 0% -> 0%
where the time goes in v1:
time: 80.2 us; the launch traced here: 80 us
  Pallas kernels  76.6 us (96%)
  between operations  1.93 us (2%)
  other arithmetic  0.88 us (1%)
    pallas_call x1, Pallas kernels, on_device(): pl.pallas_call(functools.partial(kernel, sizes), out_shape=(jax.ShapeDtyp...  76.6 us

profile of v1, /device:TPU:1, one launch (start us, length us, event | category | flops | bytes accessed | tf_op | source)
XLA Modules:
  0.0 80.0 jit_solution(7714158651920838381)
XLA Ops:
  1.9 76.6 %shard_map.68 = (bf16[144,256]{1,0:T(8,128)(2,1)S(1)}, bf16[144,1152]{1,0:T(8,128)(2,1)S(1)}) custom-call(bf16[144,256]{1,0:T(8,128)(2,1)} %image_hbm.1, bf16[1152,256]{1,0:T(8,128)(2,1)} %feat_hbm.1, bf16[144,1152]{1,0:T(8,128)(2,1)} %weight_hbm.1, f32[1]{0:T(128)S(6)} %copy.8.scale_ref, f32[1]{0:T(128)S(6)} %copy.9.bias_ref), custom_call_target="tpu_custom_call" | custom-call | tf_op jit(solution)/shard_map/pallas_call | solution.py:522
  78.5 0.9 %convert_element_type.3 = f32[144,1152]{1,0:T(8,128)} convert(bf16[144,1152]{1,0:T(8,128)(2,1)S(1)} %get-tuple-element.5) | non-fusion elementwise | flops 165888 | bytes 995328 | tf_op jit(solution)/shard_map/convert_element_type | solution.py:535
  79.4 0.6 copy.10

commit v2 on v1

--- a/solution.py
+++ b/solution.py
@@ -171,24 +171,14 @@
     for peer in greeted:
         pl.semaphore_signal(barrier, inc=1, device_id=peer, device_id_type=MESH)
 
-    turn_f[LANES:, :] = jnp.zeros((LANES, pairs), F32)
+    per = LANES // rows
     loads[0].wait()
-    turn_f[:LANES, :] = image_ref[:LANES, :].astype(F32)
-    turn_f[pl.ds(pl.multiple_of(LANES + tail * k, 16), tail), :] = image_ref[LANES:, :].astype(F32)
-    swap_src[...] = jnp.transpose(turn_f[...]).astype(BF16)
-    swap_dst[pl.ds(k, 1)] = swap_src[at16(rows * k, rows), :][None]
-    pl.semaphore_wait(barrier, len(greeted))
-
-    swaps = [
-        push(
-            swap_src.at[at16(rows * ((k + m) % n_emb), rows), :],
-            swap_dst.at[k],
-            swap_s.at[m],
-            swap_r.at[m],
-            emb_peer(m),
-        )
-        for m in range(1, n_emb)
-    ]
+    turned = jnp.transpose(image_ref[:LANES, :].astype(F32)).astype(BF16)
+    for j in range(n_emb):
+        swap_src[j, :rows, :] = turned[rows * j : rows * (j + 1)]
+        at = LANES * (j // per)
+        swap_src[j, rows:, :] = image_ref[LANES:, at : at + LANES]
+    swap_dst[pl.ds(k, 1)] = swap_src[pl.ds(k, 1)]
     own_text = at16(depth * k, depth)
     loads[1].wait()
     loads[2].wait()
@@ -196,11 +186,32 @@
         weight_ref[...], feat_ref[...], preferred_element_type=F32
     ).astype(BF16)
 
+    pl.semaphore_wait(barrier, len(greeted))
+
+    swaps = [
+        push(
+            swap_src.at[(k + m) % n_emb],
+            swap_dst.at[k],
+            swap_s.at[m],
+            swap_r.at[m],
+            emb_peer(m),
+        )
+        for m in range(1, n_emb)
+    ]
     upper, lower = line_peer(1), line_peer(n_hi - 1)
     cut = up(depth // 2, 16)
+    below_to = depth * (2 * ((hi + n_hi - 1) % n_hi) + core)
+    above_to = depth * (2 * ((hi + 1) % n_hi) + core)
+
+    def text_push(start, size, i, peer):
+        at = at16(start, size)
+        return push(text_nat.at[at, :], text_nat.at[at, :], gat_s.at[i], gat_r.at[i], peer)
+
     gathers = [
-        push(text_nat.at[own_text, :], text_nat.at[own_text, :], gat_s.at[0], gat_r.at[0], upper),
-        push(text_nat.at[own_text, :], text_nat.at[own_text, :], gat_s.at[1], gat_r.at[1], lower),
+        text_push(depth * k, cut, 0, upper),
+        text_push(depth * k + cut, depth - cut, 1, lower),
+        text_push(depth * k + cut, depth - cut, 2, upper),
+        text_push(depth * k, cut, 3, lower),
     ]
     forwards = [
         push(text_nat.at[own_text, :], text_nat.at[own_text, :], fwd_s.at[0], fwd_r.at[0], partner)
@@ -208,8 +219,10 @@
 
     for copy in swaps:
         copy.wait_recv()
-    raw = [swap_dst[j, :, :LANES].astype(F32) for j in range(n_emb)]
-    raw.append(sum(swap_dst[j, :, LANES:].astype(F32) for j in range(n_emb)))
+    raw = [swap_dst[j, :rows, :].astype(F32) for j in range(n_emb)]
+    tails = jnp.concatenate([swap_dst[j, rows:, :].astype(F32) for j in range(n_emb)], axis=0)
+    turn_f[:LANES, :LANES] = jnp.transpose(tails)
+    raw.append(turn_f[at16(rows * (k % per), rows), :LANES])
     square = sum(jnp.sum(r * r, axis=1, keepdims=True) for r in raw)
     image_inv = 1.0 / jnp.sqrt(square + EPSILON)
     home = slot(0)
@@ -229,20 +242,13 @@
     for o in (1, -1, N_X, -N_X, N_X - 1, 1 - N_X):
         pass_on(0, o)
 
-    below = at16(depth * (2 * ((hi + n_hi - 1) % n_hi) + core), depth)
-    above = at16(depth * (2 * ((hi + 1) % n_hi) + core), depth)
-    across = depth * (2 * ((hi + 2) % n_hi) + core)
-    below_cut = at16(depth * (2 * ((hi + n_hi - 1) % n_hi) + core), cut)
-    above_cut = at16(depth * (2 * ((hi + 1) % n_hi) + core) + cut, depth - cut)
     gathers[0].wait_recv()
-    gathers.append(
-        push(text_nat.at[below_cut, :], text_nat.at[below_cut, :], gat_s.at[2], gat_r.at[2], upper)
-    )
+    gathers.append(text_push(below_to, cut, 4, upper))
     gathers[1].wait_recv()
-    gathers.append(
-        push(text_nat.at[above_cut, :], text_nat.at[above_cut, :], gat_s.at[3], gat_r.at[3], lower)
-    )
-    for i, come in ((1, below), (2, above)):
+    gathers.append(text_push(above_to + cut, depth - cut, 5, lower))
+    for i, need, come in ((1, 2, below_to), (2, 3, above_to)):
+        gathers[need].wait_recv()
+        come = at16(come, depth)
         forwards.append(
             push(text_nat.at[come, :], text_nat.at[come, :], fwd_s.at[i], fwd_r.at[i], partner)
         )
@@ -252,9 +258,9 @@
         for o in (N_X + 2, N_X + 1, 2):
             pass_on(near, near * o)
 
-    gathers[2].wait_recv()
-    gathers[3].wait_recv()
-    come = at16(across, depth)
+    gathers[4].wait_recv()
+    gathers[5].wait_recv()
+    come = at16(depth * (2 * ((hi + 2) % n_hi) + core), depth)
     forwards.append(
         push(text_nat.at[come, :], text_nat.at[come, :], fwd_s.at[3], fwd_r.at[3], partner)
     )
@@ -401,10 +407,6 @@
         for m in range(1, n_group)
     ]
 
-    for way in (1, -1):
-        dirs[slot(way), :] = collect(way, (2 * way, 5 * way, 6 * way)).astype(BF16)
-        give_back(way, way)
-
     total = head_src[at16(chunk * first_group, chunk), :].astype(F32)
     for m in range(1, n_group):
         heads[m - 1].wait_recv()
@@ -414,6 +416,21 @@
         col_src[chunk:, :] = jnp.zeros((piece * n_col - chunk, LANES), BF16)
     cols = [
         push(col_src.at[at16(piece * col_of(m), piece), :], col_dst.at[m], col_s.at[m], col_r.at[m], col_peer(m))
+        for m in range(1, n_col)
+    ]
+
+    for way in (1, -1):
+        dirs[slot(way), :] = collect(way, (2 * way, 5 * way, 6 * way)).astype(BF16)
+        give_back(way, way)
+
+    own_piece = at16(piece * second_group, piece)
+    total = col_src[own_piece, :].astype(F32)
+    for m in range(1, n_col):
+        cols[m - 1].wait_recv()
+        total = total + col_dst[m].astype(F32)
+    col_sum[own_piece, :] = total.astype(BF16)
+    col_gathers = [
+        push(col_sum.at[own_piece, :], col_sum.at[own_piece, :], cga_s.at[m], cga_r.at[m], col_peer(m))
         for m in range(1, n_col)
     ]
 
@@ -433,16 +450,7 @@
     ]
     back_dst[own_rows, :] = back_src[pl.ds(k, 1)][0]
 
-    own_piece = at16(piece * second_group, piece)
-    total = col_src[own_piece, :].astype(F32)
-    for m in range(1, n_col):
-        cols[m - 1].wait_recv()
-        total = total + col_dst[m].astype(F32)
-    col_sum[own_piece, :] = total.astype(BF16)
-    col_gathers = [
-        push(col_sum.at[own_piece, :], col_sum.at[own_piece, :], cga_s.at[m], cga_r.at[m], col_peer(m))
-        for m in range(1, n_col)
-    ]
+
     for copy in col_gathers:
         copy.wait_recv()
     own_chunk = at16(chunk * first_group, chunk)
@@ -486,8 +494,8 @@
         pltpu.VMEM((width, pairs), BF16),
         pltpu.VMEM((depth, width), BF16),
         pltpu.VMEM((2 * LANES, pairs), F32),
-        pltpu.VMEM((pairs, 2 * LANES), BF16),
-        pltpu.VMEM((n_emb, rows, 2 * LANES), BF16),
+        pltpu.VMEM((n_emb, rows + depth - LANES, LANES), BF16),
+        pltpu.VMEM((n_emb, rows + depth - LANES, LANES), BF16),
         pltpu.VMEM((rows * slots, wide), BF16),
         pltpu.VMEM((depth * n_emb, pairs), BF16),
         pltpu.VMEM((wide, pairs), BF16),
@@ -510,7 +518,7 @@
         pltpu.VMEM((chunk * n_group, LANES), BF16),
     ]
     scratch.append(pltpu.SemaphoreType.DMA((3,)))
-    for count in (n_emb, slots, 4, 4, n_hi, 4, 2, slots, n_emb, n_group, n_col, n_col, n_group):
+    for count in (n_emb, slots, 6, 4, n_hi, 4, 2, slots, n_emb, n_group, n_col, n_col, n_group):
         scratch += [pltpu.SemaphoreType.DMA((count,))] * 2
     hbm = pl.BlockSpec(memory_space=pltpu.HBM)
     smem = pl.BlockSpec(memory_space=pltpu.SMEM)

time: 80.2 us -> 79.1 us (0.986)
  Pallas kernels: 76.6 us -> 75.3 us
    pallas_call x1, Pallas kernels: 76.6 us -> 75.3 us  [on_device(): pl.pallas_call(functools.partial(kernel, sizes), out_shape=(jax.ShapeDtyp...]
where the time goes in v2:
time: 79.1 us; the launch traced here: 78.8 us
  Pallas kernels  75.3 us (95%)
  between operations  1.93 us (2%)
  other arithmetic  0.88 us (1%)
    pallas_call x1, Pallas kernels, on_device(): pl.pallas_call(functools.partial(kernel, sizes), out_shape=(jax.ShapeDtyp...  75.3 us

profile of v2, /device:TPU:1, one launch (start us, length us, event | category | flops | bytes accessed | tf_op | source)
XLA Modules:
  0.0 78.8 jit_solution(3448674732023633764)
XLA Ops:
  1.9 75.3 %shard_map.68 = (bf16[144,256]{1,0:T(8,128)(2,1)S(1)}, bf16[144,1152]{1,0:T(8,128)(2,1)S(1)}) custom-call(bf16[144,256]{1,0:T(8,128)(2,1)} %image_hbm.1, bf16[1152,256]{1,0:T(8,128)(2,1)} %feat_hbm.1, bf16[144,1152]{1,0:T(8,128)(2,1)} %weight_hbm.1, f32[1]{0:T(128)S(6)} %copy.8.scale_ref, f32[1]{0:T(128)S(6)} %copy.9.bias_ref), custom_call_target="tpu_custom_call" | custom-call | tf_op jit(solution)/shard_map/pallas_call | solution.py:530
  77.3 0.9 %convert_element_type.3 = f32[144,1152]{1,0:T(8,128)} convert(bf16[144,1152]{1,0:T(8,128)(2,1)S(1)} %get-tuple-element.5) | non-fusion elementwise | flops 165888 | bytes 995328 | tf_op jit(solution)/shard_map/convert_element_type | solution.py:543
  78.1 0.6 copy.10

commit v3 on v2

--- a/solution.py
+++ b/solution.py
@@ -116,8 +116,10 @@
     def chip_at(plane, line):
         return (plane // N_X) * (N_X * N_Y) + line * N_X + plane % N_X
 
+    plane_step = {4: 2, 3: 6, 5: 3, 2: 5, 6: 1, 1: 7, 7: 4}
+
     def group_of(m):
-        return (first_group + m) % n_group
+        return (first_group + plane_step[m] * (1 - core) + m * core) % n_group
 
     def group_peer(m):
         to = group_of(m)
@@ -125,7 +127,7 @@
         return (here * (1 - core) + there * core, k)
 
     def col_of(m):
-        return (second_group + m) % n_col
+        return (second_group + m * (1 - core) + plane_step[m] * core) % n_col
 
     def col_peer(m):
         to = col_of(m)
@@ -147,6 +149,9 @@
         copy.start()
         return copy
 
+    def far_first(n):
+        return sorted(range(1, n), key=lambda m: -min(m, n - m))
+
     def slot(o):
         return pl.ds(rows * SLOT[o], rows)
 
@@ -162,7 +167,7 @@
     ]
 
     greeted = (
-        [emb_peer(m) for m in (4, 3, 5, 2, 6, 1, 7)]
+        [emb_peer(m) for m in far_first(n_emb)]
         + [dp_peer(o) for o in (1, -1, N_X, -N_X, N_X - 1, 1 - N_X, N_X + 1, -N_X - 1)]
         + [group_peer(m) for m in range(1, n_group)]
         + [col_peer(m) for m in range(1, n_col)]
@@ -196,7 +201,7 @@
             swap_r.at[m],
             emb_peer(m),
         )
-        for m in range(1, n_emb)
+        for m in far_first(n_emb)
     ]
     upper, lower = line_peer(1), line_peer(n_hi - 1)
     cut = up(depth // 2, 16)
@@ -308,9 +313,31 @@
             images[at, :], weights[at, :], (((0,), (0,)), ((), ())), preferred_element_type=F32
         )
 
+    returns = {}
+
+    def give_back(o, step):
+        returns[o] = push(
+            dirs.at[slot(o), :],
+            dirs_back.at[slot(o), :],
+            ret_s.at[SLOT[o]],
+            ret_r.at[SLOT[o]],
+            dp_peer(step),
+        )
+
+    def collect(o, sources):
+        value = dirs[slot(o), :].astype(F32)
+        for source in sources:
+            returns[source].wait_recv()
+            value = value + dirs_back[slot(source), :].astype(F32)
+        return value
+
     for o in ORDER[3:NEAR]:
         window[o].wait_recv()
     inner = meet(0, NEAR)
+    turn_back(0, NEAR)
+    for way in (1, -1):
+        give_back(4 * way, N_X * way)
+        give_back(3 * way, (N_X - 1) * way)
     for o in ORDER[NEAR:MIDDLE]:
         window[o].wait_recv()
     inner = inner + meet(NEAR, MIDDLE)
@@ -330,25 +357,7 @@
         theirs = at16(depth * (2 * hi_of(m) + 1 - core), depth)
         paired[m] = push(text_part.at[theirs, :], pair_dst.at[m], pair_s.at[m], pair_r.at[m], partner)
 
-    turn_back(0, len(ORDER))
-    returns = {}
-
-    def give_back(o, step):
-        returns[o] = push(
-            dirs.at[slot(o), :],
-            dirs_back.at[slot(o), :],
-            ret_s.at[SLOT[o]],
-            ret_r.at[SLOT[o]],
-            dp_peer(step),
-        )
-
-    def collect(o, sources):
-        value = dirs[slot(o), :].astype(F32)
-        for source in sources:
-            returns[source].wait_recv()
-            value = value + dirs_back[slot(source), :].astype(F32)
-        return value
-
+    turn_back(NEAR, len(ORDER))
     def summed(m):
         paired[m].wait_recv()
         mine = at16(depth * (2 * hi_of(m) + core), depth)
@@ -377,10 +386,8 @@
     lines.append(line(2, 3, second, lower))
     for way in (1, -1):
         give_back(5 * way, N_X * way)
-        give_back(3 * way, (N_X - 1) * way)
         give_back(6 * way, (N_X + 1) * way)
         give_back(2 * way, way)
-        give_back(4 * way, N_X * way)
     for copy in swaps + gathers + forwards + list(window.values()):
         copy.wait_send()
     total = summed(0)
@@ -404,19 +411,19 @@
             head_r.at[m],
             group_peer(m),
         )
-        for m in range(1, n_group)
+        for m in far_first(n_group)
     ]
 
     total = head_src[at16(chunk * first_group, chunk), :].astype(F32)
-    for m in range(1, n_group):
-        heads[m - 1].wait_recv()
+    for m, copy in zip(far_first(n_group), heads):
+        copy.wait_recv()
         total = total + head_dst[m].astype(F32)
     col_src[:chunk, :] = total.astype(BF16)
     if piece * n_col > chunk:
         col_src[chunk:, :] = jnp.zeros((piece * n_col - chunk, LANES), BF16)
     cols = [
         push(col_src.at[at16(piece * col_of(m), piece), :], col_dst.at[m], col_s.at[m], col_r.at[m], col_peer(m))
-        for m in range(1, n_col)
+        for m in far_first(n_col)
     ]
 
     for way in (1, -1):
@@ -425,13 +432,13 @@
 
     own_piece = at16(piece * second_group, piece)
     total = col_src[own_piece, :].astype(F32)
-    for m in range(1, n_col):
-        cols[m - 1].wait_recv()
+    for m, copy in zip(far_first(n_col), cols):
+        copy.wait_recv()
         total = total + col_dst[m].astype(F32)
     col_sum[own_piece, :] = total.astype(BF16)
     col_gathers = [
         push(col_sum.at[own_piece, :], col_sum.at[own_piece, :], cga_s.at[m], cga_r.at[m], col_peer(m))
-        for m in range(1, n_col)
+        for m in far_first(n_col)
     ]
 
     for copy in lines + list(paired.values()) + heads:
@@ -446,7 +453,7 @@
     own_rows = at16(rows * k, rows)
     backs = [
         push(back_src.at[(k + m) % n_emb], back_dst.at[own_rows, :], back_s.at[m], back_r.at[m], emb_peer(m))
-        for m in range(1, n_emb)
+        for m in far_first(n_emb)
     ]
     back_dst[own_rows, :] = back_src[pl.ds(k, 1)][0]
 
@@ -457,7 +464,7 @@
     head_sum[own_chunk, :] = col_sum[:chunk, :]
     head_gathers = [
         push(col_sum.at[pl.ds(0, chunk), :], head_sum.at[own_chunk, :], hga_s.at[m], hga_r.at[m], group_peer(m))
-        for m in range(1, n_group)
+        for m in far_first(n_group)
     ]
 
     for copy in backs:

time: 79.1 us -> 76.7 us (0.970)
  Pallas kernels: 75.3 us -> 73.1 us
    pallas_call x1, Pallas kernels: 75.3 us -> 73.1 us  [on_device(): pl.pallas_call(functools.partial(kernel, sizes), out_shape=(jax.ShapeDtyp...]
where the time goes in v3:
time: 76.7 us; the launch traced here: 76.6 us
  Pallas kernels  73.1 us (95%)
  between operations  1.93 us (3%)
  other arithmetic  0.88 us (1%)
    pallas_call x1, Pallas kernels, on_device(): pl.pallas_call(functools.partial(kernel, sizes), out_shape=(jax.ShapeDtyp...  73.1 us

profile of v3, /device:TPU:1, one launch (start us, length us, event | category | flops | bytes accessed | tf_op | source)
XLA Modules:
  0.0 76.6 jit_solution(11198029695242304212)
XLA Ops:
  1.9 73.1 %shard_map.68 = (bf16[144,256]{1,0:T(8,128)(2,1)S(1)}, bf16[144,1152]{1,0:T(8,128)(2,1)S(1)}) custom-call(bf16[144,256]{1,0:T(8,128)(2,1)} %image_hbm.1, bf16[1152,256]{1,0:T(8,128)(2,1)} %feat_hbm.1, bf16[144,1152]{1,0:T(8,128)(2,1)} %weight_hbm.1, f32[1]{0:T(128)S(6)} %copy.8.scale_ref, f32[1]{0:T(128)S(6)} %copy.9.bias_ref), custom_call_target="tpu_custom_call" | custom-call | tf_op jit(solution)/shard_map/pallas_call | solution.py:537
  75.1 0.9 %convert_element_type.3 = f32[144,1152]{1,0:T(8,128)} convert(bf16[144,1152]{1,0:T(8,128)(2,1)S(1)} %get-tuple-element.5) | non-fusion elementwise | flops 165888 | bytes 995328 | tf_op jit(solution)/shard_map/convert_element_type | solution.py:550
  75.9 0.6 copy.10

commit v4 on v3

--- a/solution.py
+++ b/solution.py
@@ -341,6 +341,10 @@
     for o in ORDER[NEAR:MIDDLE]:
         window[o].wait_recv()
     inner = inner + meet(NEAR, MIDDLE)
+    turn_back(NEAR, MIDDLE)
+    for way in (1, -1):
+        give_back(5 * way, N_X * way)
+        give_back(2 * way, way)
     grad[...] = text_side(0, MIDDLE)
     for o in ORDER[MIDDLE:]:
         window[o].wait_recv()
@@ -357,7 +361,8 @@
         theirs = at16(depth * (2 * hi_of(m) + 1 - core), depth)
         paired[m] = push(text_part.at[theirs, :], pair_dst.at[m], pair_s.at[m], pair_r.at[m], partner)
 
-    turn_back(NEAR, len(ORDER))
+    turn_back(MIDDLE, len(ORDER))
+
     def summed(m):
         paired[m].wait_recv()
         mine = at16(depth * (2 * hi_of(m) + core), depth)
@@ -385,9 +390,7 @@
     line_src[2, cut:, :] = (falling[cut:] + mid_dst[cut:, :].astype(F32)).astype(BF16)
     lines.append(line(2, 3, second, lower))
     for way in (1, -1):
-        give_back(5 * way, N_X * way)
         give_back(6 * way, (N_X + 1) * way)
-        give_back(2 * way, way)
     for copy in swaps + gathers + forwards + list(window.values()):
         copy.wait_send()
     total = summed(0)

time: 76.7 us -> 75.3 us (0.982)
  Pallas kernels: 73.1 us -> 71.6 us
    pallas_call x1, Pallas kernels: 73.1 us -> 71.6 us  [on_device(): pl.pallas_call(functools.partial(kernel, sizes), out_shape=(jax.ShapeDtyp...]
where the time goes in v4:
time: 75.3 us; the launch traced here: 75 us
  Pallas kernels  71.6 us (95%)
  between operations  1.93 us (3%)
  other arithmetic  0.88 us (1%)
    pallas_call x1, Pallas kernels, on_device(): pl.pallas_call(functools.partial(kernel, sizes), out_shape=(jax.ShapeDtyp...  71.6 us

profile of v4, /device:TPU:1, one launch (start us, length us, event | category | flops | bytes accessed | tf_op | source)
XLA Modules:
  0.0 75.0 jit_solution(1201072003261301157)
XLA Ops:
  1.9 71.6 %shard_map.68 = (bf16[144,256]{1,0:T(8,128)(2,1)S(1)}, bf16[144,1152]{1,0:T(8,128)(2,1)S(1)}) custom-call(bf16[144,256]{1,0:T(8,128)(2,1)} %image_hbm.1, bf16[1152,256]{1,0:T(8,128)(2,1)} %feat_hbm.1, bf16[144,1152]{1,0:T(8,128)(2,1)} %weight_hbm.1, f32[1]{0:T(128)S(6)} %copy.8.scale_ref, f32[1]{0:T(128)S(6)} %copy.9.bias_ref), custom_call_target="tpu_custom_call" | custom-call | tf_op jit(solution)/shard_map/pallas_call | solution.py:540
  73.5 0.9 %convert_element_type.3 = f32[144,1152]{1,0:T(8,128)} convert(bf16[144,1152]{1,0:T(8,128)(2,1)S(1)} %get-tuple-element.5) | non-fusion elementwise | flops 165888 | bytes 995328 | tf_op jit(solution)/shard_map/convert_element_type | solution.py:553
  74.4 0.6 copy.10

commit v5 on v4

--- a/solution.py
+++ b/solution.py
@@ -362,6 +362,8 @@
         paired[m] = push(text_part.at[theirs, :], pair_dst.at[m], pair_s.at[m], pair_r.at[m], partner)
 
     turn_back(MIDDLE, len(ORDER))
+    for way in (1, -1):
+        give_back(6 * way, (N_X + 1) * way)
 
     def summed(m):
         paired[m].wait_recv()
@@ -389,8 +391,6 @@
     lines[1].wait_recv()
     line_src[2, cut:, :] = (falling[cut:] + mid_dst[cut:, :].astype(F32)).astype(BF16)
     lines.append(line(2, 3, second, lower))
-    for way in (1, -1):
-        give_back(6 * way, (N_X + 1) * way)
     for copy in swaps + gathers + forwards + list(window.values()):
         copy.wait_send()
     total = summed(0)

time: 75.3 us -> 75.1 us (level)
  the two profiles are of different devices: /device:TPU:1 before, /device:TPU:128 now
where the time goes in v5:
time: 75.1 us; the launch traced here: 74.9 us
  Pallas kernels  71.5 us (95%)
  between operations  1.93 us (3%)
  other arithmetic  0.88 us (1%)
    pallas_call x1, Pallas kernels, on_device(): pl.pallas_call(functools.partial(kernel, sizes), out_shape=(jax.ShapeDtyp...  71.5 us

profile of v5, /device:TPU:128, one launch (start us, length us, event | category | flops | bytes accessed | tf_op | source)
XLA Modules:
  0.0 74.9 jit_solution(9651177504437464801)
XLA Ops:
  1.9 71.5 %shard_map.68 = (bf16[144,256]{1,0:T(8,128)(2,1)S(1)}, bf16[144,1152]{1,0:T(8,128)(2,1)S(1)}) custom-call(bf16[144,256]{1,0:T(8,128)(2,1)} %image_hbm.1, bf16[1152,256]{1,0:T(8,128)(2,1)} %feat_hbm.1, bf16[144,1152]{1,0:T(8,128)(2,1)} %weight_hbm.1, f32[1]{0:T(128)S(6)} %copy.8.scale_ref, f32[1]{0:T(128)S(6)} %copy.9.bias_ref), custom_call_target="tpu_custom_call" | custom-call | tf_op jit(solution)/shard_map/pallas_call | solution.py:540
  73.4 0.9 %convert_element_type.3 = f32[144,1152]{1,0:T(8,128)} convert(bf16[144,1152]{1,0:T(8,128)(2,1)S(1)} %get-tuple-element.5) | non-fusion elementwise | flops 165888 | bytes 995328 | tf_op jit(solution)/shard_map/convert_element_type | solution.py:553
  74.3 0.6 copy.10
